TPU v7x, 512 devices: a whole 4x8x8 slice. The times are simulated.
512 devices in a mesh: ax: 32 (over x, y), tr: 16 (over z, core).
Axes of the slice: x: 4, y: 8, z: 8, core: 2. Of those that a mesh axis runs over, the one named last changes fastest.
Arguments:
- solid_old: float32 [512, 512, 512], P('ax', 'tr'), may hold values from -6 to 6
- gas_rate: bfloat16 [512, 512, 512], P('ax', 'tr'), may hold values from 0 to 1, as said below
- gas_inlet: float32 [512, 512], P('tr'), may hold values from -6 to 6
Outputs:
- gas_new: float32 [512, 512, 512], P('ax', 'tr')
- solid_new: float32 [512, 512, 512], P('ax', 'tr')
- temperature_gap: float32 [512, 512, 512], P('ax', 'tr')
Inputs may be any that keep to these rules, and one draw needn't show every extreme that they name: `gas_rate`: positive transfer numbers.
All inputs are finite; a program needn't handle non-finite values.
Results may differ from a plain program's by a relative error of at most 0.0013.
Values sent between devices are 32-bit elements; how exact they have to be, the bound alone decides.
A program may use at most 64 MiB of HBM per device.

v0:
```python
import functools
import math

import jax
import jax.numpy as jnp
import ml_dtypes
import numpy as np
from jax import lax
from jax.experimental import pallas as pl
from jax.experimental.pallas import tpu as pltpu
from jax.sharding import PartitionSpec as P

COUPLE = 8.0
ALONG_ROW = 100.0
ACROSS_ROWS = 4000.0
MESH = pl.DeviceIdType.MESH
F32 = jnp.float32
BF16 = jnp.bfloat16


def halves(table):
    high = table.astype(np.float32).astype(ml_dtypes.bfloat16)
    low = (table - high.astype(np.float64)).astype(np.float32).astype(ml_dtypes.bfloat16)
    return np.stack([high, low])


def line_inverse(order_n, conduct):
    theta = 2.0 * math.asinh(0.5 / math.sqrt(conduct))
    i = np.arange(1, order_n + 1, dtype=np.float64)
    near = np.minimum(i[:, None], i[None, :])
    far = order_n + 1 - np.maximum(i[:, None], i[None, :])
    return np.sinh(near * theta) * np.sinh(far * theta) / (
        conduct * math.sinh(theta) * math.sinh((order_n + 1) * theta)
    )


class Across:
    def __init__(self, rows, blocks, conduct, group):
        theta = 2.0 * math.asinh(0.5 / math.sqrt(conduct))
        self.kappa = 1.0 / (2.0 * conduct * math.sinh(theta))
        self.step = math.exp(-rows * theta)
        self.end = math.exp(-(rows * blocks + 1) * theta)
        self.reflect = -self.kappa * math.exp(-theta) / (1.0 - self.end**2)
        a = np.arange(1, rows + 1, dtype=np.float64)
        block = self.kappa * np.exp(-np.abs(a[:, None] - a[None, :]) * theta)
        self.local = halves(np.kron(np.eye(group), block))
        weights = np.stack(
            [
                np.exp(-(rows - a) * theta),
                np.exp(-(a - 1) * theta),
                np.exp(-a * theta),
                np.exp(-(rows + 1 - a) * theta),
            ]
        )
        self.weights = np.repeat(weights[:, :, None], 128, axis=2).astype(np.float32)


def dot3(a_high, a_low, b_high, b_low):
    dot = functools.partial(jnp.dot, preferred_element_type=F32)
    return dot(a_high, b_high) + (dot(a_low, b_high) + dot(a_high, b_low))


def split(value):
    high = value.astype(BF16)
    return high, (value - high.astype(F32)).astype(BF16)


def exchange_kernel(
    n_ax,
    n_tr,
    across,
    solid_hbm,
    rate_hbm,
    inlet_hbm,
    along_hbm,
    local_hbm,
    weights_hbm,
    gas_hbm,
    part_hbm,
    carry_out,
    solid,
    rate,
    inlet,
    along,
    local,
    weights,
    cumul,
    particular,
    gas,
    right_hi,
    right_lo,
    mid_hi,
    mid_lo,
    part,
    pieces,
    first,
    maps,
    flows,
    inflows,
    inflow,
    sums,
    sums_in,
    ends,
    ends_in,
    load_sem,
    store_sem,
    send_sem,
    recv_sem,
):
    me_ax = lax.axis_index("ax")
    me_tr = lax.axis_index("tr")
    planes, rows, cols = solid.shape
    col_tiles = cols // 128

    loads = [
        pltpu.make_async_copy(source, target, load_sem.at[i])
        for i, (source, target) in enumerate(
            [
                (rate_hbm, rate),
                (solid_hbm, solid),
                (inlet_hbm, inlet),
                (weights_hbm, weights),
                (local_hbm, local),
                (along_hbm, along),
            ]
        )
    ]
    for load in loads:
        load.start()

    barrier = pltpu.get_barrier_semaphore()

    def greet_ax(k, _):
        pl.semaphore_signal(
            barrier, inc=1, device_id=(lax.rem(me_ax + k, n_ax), me_tr), device_id_type=MESH
        )
        return 0

    def greet_tr(k, _):
        pl.semaphore_signal(
            barrier, inc=1, device_id=(me_ax, lax.rem(me_tr + k, n_tr)), device_id_type=MESH
        )
        return 0

    lax.fori_loop(1, n_ax, greet_ax, 0)
    lax.fori_loop(1, n_tr, greet_tr, 0)

    for load in loads[:3]:
        load.wait()

    upper = lax.broadcasted_iota(jnp.int32, (8, 128), 0) < 4

    def group_maps(g, _):
        at = pl.ds(pl.multiple_of(g * 16, 16), 16)

        def plane(p, state):
            factor, offset = state
            r = rate[p, at, :].astype(F32)
            keep = 1.0 / (1.0 + r)
            factor = factor * keep
            offset = offset * keep + r * solid[p, at, :] * keep
            cumul[p, at, :] = factor
            particular[p, at, :] = offset
            return factor, offset

        factor, offset = lax.fori_loop(
            0,
            planes,
            plane,
            (jnp.ones((16, cols), F32), jnp.zeros((16, cols), F32)),
            unroll=True,
        )
        start = inlet[at, :]
        for h in range(2):
            for c in range(col_tiles):
                box = (slice(8 * h, 8 * h + 8), slice(128 * c, 128 * c + 128))
                f, o, s = factor[box], offset[box], start[box]
                q = (g * 2 + h) * (2 * col_tiles) + 2 * c
                pieces[q] = jnp.where(upper, f, pltpu.roll(o, 4, 0))
                pieces[q + 1] = jnp.where(upper, pltpu.roll(f, 4, 0), o)
                first[q] = s
                first[q + 1] = pltpu.roll(s, 4, 0)
        return 0

    lax.fori_loop(0, rows // 16, group_maps, 0)

    pl.semaphore_wait(barrier, n_ax - 1 + n_tr - 1)

    def send_map(k, _):
        to = lax.rem(me_ax + k, n_ax)
        pltpu.make_async_remote_copy(
            src_ref=pieces.at[to],
            dst_ref=maps.at[me_ax],
            send_sem=send_sem.at[0],
            recv_sem=recv_sem.at[0],
            device_id=(to, me_tr),
            device_id_type=MESH,
        ).start()
        return 0

    lax.fori_loop(1, n_ax, send_map, 0)
    maps[me_ax] = pieces[me_ax]

    def wait_for(ref, count, sem):
        box = ref.at[pl.ds(0, count)]
        pltpu.make_async_copy(box, box, sem).wait()

    wait_for(maps, n_ax - 1, recv_sem.at[0])

    def march(k, state):
        flows[k] = state[:4]
        m = maps[k]
        return m * state + pltpu.roll(m, 4, 0)

    lax.fori_loop(0, n_ax, march, first[me_ax], unroll=True)

    def send_flow(k, _):
        to = lax.rem(me_ax + k, n_ax)
        pltpu.make_async_remote_copy(
            src_ref=flows.at[to],
            dst_ref=inflows.at[me_ax],
            send_sem=send_sem.at[1],
            recv_sem=recv_sem.at[1],
            device_id=(to, me_tr),
            device_id_type=MESH,
        ).start()
        return 0

    lax.fori_loop(1, n_ax, send_flow, 0)
    inflows[me_ax] = flows[me_ax]
    loads[3].wait()
    wait_for(inflows, n_ax - 1, recv_sem.at[1])

    for h in range(rows // 8):
        for c in range(col_tiles):
            q = h * 2 * col_tiles + 2 * c
            inflow[8 * h : 8 * h + 8, 128 * c : 128 * c + 128] = jnp.concatenate(
                [inflows[q], inflows[q + 1]], axis=0
            )

    def plane_group(g, _):
        for c in range(col_tiles):
            lanes = pl.ds(128 * c, 128)
            to_last, to_first = weights[0], weights[1]
            totals = []
            for j in range(4):
                p = g * 4 + j
                s = solid[p, :, lanes]
                r = rate[p, :, lanes].astype(F32)
                new = particular[p, :, lanes] + cumul[p, :, lanes] * inflow[:, lanes]
                gas[p, :, lanes] = new
                right = s + (COUPLE * r) * (new - s)
                at = pl.ds(pl.multiple_of(p * rows, rows), rows)
                right_hi[at, lanes], right_lo[at, lanes] = split(right)
                totals.append(
                    (
                        jnp.sum(right * to_last, axis=0, keepdims=True),
                        jnp.sum(right * to_first, axis=0, keepdims=True),
                    )
                )
            sums[g * col_tiles + c] = jnp.concatenate(
                [t[0] for t in totals] + [t[1] for t in totals], axis=0
            )
        return 0

    lax.fori_loop(0, planes // 4, plane_group, 0)

    def send_sum(k, _):
        to = lax.rem(me_tr + k, n_tr)
        pltpu.make_async_remote_copy(
            src_ref=sums.at[to],
            dst_ref=sums_in.at[me_tr],
            send_sem=send_sem.at[2],
            recv_sem=recv_sem.at[2],
            device_id=(me_ax, to),
            device_id_type=MESH,
        ).start()
        return 0

    lax.fori_loop(1, n_tr, send_sum, 0)
    sums_in[me_tr] = sums[me_tr]

    gas_copy = pltpu.make_async_copy(gas, gas_hbm, store_sem.at[0])
    gas_copy.start()

    loads[4].wait()
    group = local.shape[1]

    def local_solve(g, _):
        at = pl.ds(pl.multiple_of(g * group, group), group)
        mid = dot3(local[0], local[1], right_hi[at, :], right_lo[at, :])
        mid_hi[at, :], mid_lo[at, :] = split(mid)
        return 0

    lax.fori_loop(0, planes * rows // group, local_solve, 0)

    wait_for(sums_in, n_tr - 1, recv_sem.at[2])

    forward = [jnp.zeros((8, 128), F32)]
    for d in range(n_tr):
        forward.append(across.step * forward[-1] + sums_in[d])
    backward = [jnp.zeros((8, 128), F32)]
    for d in reversed(range(n_tr)):
        backward.append(across.step * backward[-1] + sums_in[d])
    whole = jnp.where(upper, forward[-1], backward[-1])
    mirror = across.reflect * (pltpu.roll(whole, 4, 0) - across.end * whole)
    for d in range(n_tr):
        inner = jnp.where(upper, forward[d], backward[n_tr - 1 - d])
        fade = jnp.where(upper, across.step**d, across.step ** (n_tr - 1 - d))
        ends[d] = across.kappa * inner + mirror * fade

    def ends_box(owner):
        return ends_in.at[
            pl.ds(pl.multiple_of(owner // col_tiles * 8, 8), 8),
            pl.ds(pl.multiple_of(lax.rem(owner, col_tiles) * 128, 128), 128),
        ]

    def send_end(k, _):
        to = lax.rem(me_tr + k, n_tr)
        pltpu.make_async_remote_copy(
            src_ref=ends.at[to],
            dst_ref=ends_box(me_tr),
            send_sem=send_sem.at[3],
            recv_sem=recv_sem.at[3],
            device_id=(me_ax, to),
            device_id_type=MESH,
        ).start()
        return 0

    lax.fori_loop(1, n_tr, send_end, 0)
    ends_box(me_tr)[...] = ends[me_tr]

    loads[5].wait()

    def along_solve(g, _):
        at = pl.ds(pl.multiple_of(g * group, group), group)
        part[at, :] = dot3(mid_hi[at, :], mid_lo[at, :], along[0], along[1])
        return 0

    lax.fori_loop(0, planes * rows // group, along_solve, 0)
    part_copy = pltpu.make_async_copy(part, part_hbm, store_sem.at[1])
    part_copy.start()

    wait_for(ends, n_tr - 1, recv_sem.at[3])
    end_hi, end_lo = split(ends_in[...])
    carry_out[...] = dot3(end_hi, end_lo, along[0], along[1])

    gas_copy.wait()
    part_copy.wait()
    wait_for(pieces, n_ax - 1, send_sem.at[0])
    wait_for(flows, n_ax - 1, send_sem.at[1])
    wait_for(sums, n_tr - 1, send_sem.at[2])
    wait_for(ends, n_tr - 1, send_sem.at[3])


def finish_kernel(gas_in, part, carry, weights, gas_out, solid_out, gap_out):
    rows = part.shape[1]
    cols = part.shape[2]
    lanes_of = cols // 128
    before = jnp.concatenate([weights[2]] * lanes_of, axis=1)
    after = jnp.concatenate([weights[3]] * lanes_of, axis=1)
    for j in range(4):
        new = gas_in[j]
        solid = part[j] + (
            before * jnp.broadcast_to(carry[j : j + 1, :], (rows, cols))
            + after * jnp.broadcast_to(carry[4 + j : 5 + j, :], (rows, cols))
        )
        gas_out[j] = new
        solid_out[j] = solid
        gap_out[j] = new - solid


def per_device(n_ax, n_tr, solid_old, gas_rate, gas_inlet):
    planes, rows, cols = solid_old.shape
    across = Across(rows, n_tr, ACROSS_ROWS, 8)
    along = halves(line_inverse(cols, ALONG_ROW).T)
    weights = jnp.asarray(across.weights)
    tiles = cols // 128
    anywhere = pl.BlockSpec(memory_space=pl.ANY)
    cells = planes * rows
    gas, part, carry = pl.pallas_call(
        functools.partial(exchange_kernel, n_ax, n_tr, across),
        out_shape=(
            jax.ShapeDtypeStruct((planes, rows, cols), F32),
            jax.ShapeDtypeStruct((cells, cols), F32),
            jax.ShapeDtypeStruct((planes // 4 * 8, cols), F32),
        ),
        in_specs=[anywhere] * 6,
        out_specs=(anywhere, anywhere, pl.BlockSpec(memory_space=pltpu.VMEM)),
        scratch_shapes=[
            pltpu.VMEM((planes, rows, cols), F32),
            pltpu.VMEM((planes, rows, cols), BF16),
            pltpu.VMEM((rows, cols), F32),
            pltpu.VMEM((2, cols, cols), BF16),
            pltpu.VMEM(across.local.shape, BF16),
            pltpu.VMEM((4, rows, 128), F32),
            pltpu.VMEM((planes, rows, cols), F32),
            pltpu.VMEM((planes, rows, cols), F32),
            pltpu.VMEM((planes, rows, cols), F32),
            pltpu.VMEM((cells, cols), BF16),
            pltpu.VMEM((cells, cols), BF16),
            pltpu.VMEM((cells, cols), BF16),
            pltpu.VMEM((cells, cols), BF16),
            pltpu.VMEM((cells, cols), F32),
            pltpu.VMEM((n_ax, 8, 128), F32),
            pltpu.VMEM((n_ax, 8, 128), F32),
            pltpu.VMEM((n_ax, 8, 128), F32),
            pltpu.VMEM((n_ax, 4, 128), F32),
            pltpu.VMEM((n_ax, 4, 128), F32),
            pltpu.VMEM((rows, cols), F32),
            pltpu.VMEM((n_tr, 8, 128), F32),
            pltpu.VMEM((n_tr, 8, 128), F32),
            pltpu.VMEM((n_tr, 8, 128), F32),
            pltpu.VMEM((planes // 4 * 8, cols), F32),
            pltpu.SemaphoreType.DMA((6,)),
            pltpu.SemaphoreType.DMA((2,)),
            pltpu.SemaphoreType.DMA((4,)),
            pltpu.SemaphoreType.DMA((4,)),
        ],
        compiler_params=pltpu.CompilerParams(
            collective_id=0, has_side_effects=True, vmem_limit_bytes=32 * 2**20
        ),
        name="exchange",
    )(solid_old, gas_rate, gas_inlet, jnp.asarray(along), jnp.asarray(across.local), weights)

    field = pl.BlockSpec((4, rows, cols), lambda g: (g, 0, 0))
    shape = jax.ShapeDtypeStruct((planes, rows, cols), F32)
    return pl.pallas_call(
        finish_kernel,
        grid=(planes // 4,),
        out_shape=(shape, shape, shape),
        in_specs=[
            field,
            field,
            pl.BlockSpec((8, cols), lambda g: (g, 0)),
            pl.BlockSpec((4, rows, 128), lambda g: (0, 0, 0)),
        ],
        out_specs=(field, field, field),
        compiler_params=pltpu.CompilerParams(vmem_limit_bytes=32 * 2**20),
        name="finish",
    )(gas, part.reshape(planes, rows, cols), carry, weights)


def solution(mesh):
    n_ax, n_tr = mesh.shape["ax"], mesh.shape["tr"]
    return jax.shard_map(
        functools.partial(per_device, n_ax, n_tr),
        mesh=mesh,
        in_specs=(P("ax", "tr", None), P("ax", "tr", None), P("tr", None)),
        out_specs=(P("ax", "tr", None), P("ax", "tr", None), P("ax", "tr", None)),
        check_vma=False,
    )
```

profile of v0, /device:TPU:1, one launch (start us, length us, event | category | flops | bytes accessed | tf_op | source)
XLA Modules:
  0.0 49.6 jit_solution(16559084011628928901)
XLA Ops:
  0.6 0.0 copy-start
  0.6 1.2 %copy-done = f32[16,32,512]{2,1,0:T(8,128)S(1)} copy-done((f32[16,32,512]{2,1,0:T(8,128)S(1)}, f32[16,32,512]{2,1,0:T(8,128)}, u32[]{:S(2)}) %copy-start) | copy-done | bytes 1048600
  1.9 0.0 copy-start.1
  1.9 1.2 %copy-done.1 = bf16[2,512,512]{2,1,0:T(8,128)(2,1)S(1)} copy-done((bf16[2,512,512]{2,1,0:T(8,128)(2,1)S(1)}, bf16[2,512,512]{2,1,0:T(8,128)(2,1)}, u32[]{:S(2)}) %copy-start.1) | copy-done | bytes 1048600
  3.1 0.0 copy-start.2
  3.1 1.0 %copy-done.2 = bf16[16,32,512]{2,1,0:T(8,128)(2,1)S(1)} copy-done((bf16[16,32,512]{2,1,0:T(8,128)(2,1)S(1)}, bf16[16,32,512]{2,1,0:T(8,128)(2,1)}, u32[]{:S(2)}) %copy-start.2) | copy-done | bytes 524312
  4.1 0.0 copy-start.3
  4.1 0.9 %copy-done.3 = bf16[2,256,256]{2,1,0:T(8,128)(2,1)S(1)} copy-done((bf16[2,256,256]{2,1,0:T(8,128)(2,1)S(1)}, bf16[2,256,256]{2,1,0:T(8,128)(2,1)}, u32[]{:S(2)}) %copy-start.3) | copy-done | bytes 262168
  5.1 0.0 copy-start.4
  5.1 0.8 %copy-done.4 = f32[4,32,128]{2,1,0:T(8,128)S(1)} copy-done((f32[4,32,128]{2,1,0:T(8,128)S(1)}, f32[4,32,128]{2,1,0:T(8,128)}, u32[]{:S(2)}) %copy-start.4) | copy-done | bytes 65560
  5.9 0.0 copy-start.5
  5.9 0.8 %copy-done.5 = f32[32,512]{1,0:T(8,128)S(1)} copy-done((f32[32,512]{1,0:T(8,128)S(1)}, f32[32,512]{1,0:T(8,128)}, u32[]{:S(2)}) %copy-start.5) | copy-done | bytes 65560
  6.8 40.6 %exchange.1 = (f32[16,32,512]{2,1,0:T(8,128)S(1)}, f32[512,512]{1,0:T(8,128)S(1)}, f32[32,512]{1,0:T(8,128)S(1)}) custom-call(f32[16,32,512]{2,1,0:T(8,128)S(1)} %copy-done, bf16[16,32,512]{2,1,0:T(8,128)(2,1)S(1)} %copy-done.2, f32[32,512]{1,0:T(8,128)S(1)} %copy-done.5, bf16[2,512,512]{2,1,0:T(8,128)(2,1)S(1)} %copy-done.1, ...), custom_call_target="tpu_custom_call" | custom-call | tf_op jit(solution)/shard_map/exchange/pallas_call | solution.py:381
  47.4 2.2 %finish.1 = (f32[16,32,512]{2,1,0:T(8,128)}, f32[16,32,512]{2,1,0:T(8,128)}, f32[16,32,512]{2,1,0:T(8,128)}) custom-call(f32[16,32,512]{2,1,0:T(8,128)S(1)} %get-tuple-element.6.gas_in, f32[16,32,512]{2,1,0:T(8,128)S(1)} %bitcast.1, f32[32,512]{1,0:T(8,128)S(1)} %get-tuple-element.8.carry, f32[4,32,128]{2,1,0:T(8,128)S(1)} %copy-done.4), custom_call_target="tpu_custom_call" | custom-call | tf_op jit(solution)/shard_map/finish/pallas_call | solution.py:428
Async XLA Ops:
  0.6 1.2 %copy-start = (f32[16,32,512]{2,1,0:T(8,128)S(1)}, f32[16,32,512]{2,1,0:T(8,128)}, u32[]{:S(2)}) copy-start(f32[16,32,512]{2,1,0:T(8,128)} %solid_hbm.1) | copy-start | bytes 3145732
  1.9 1.2 %copy-start.1 = (bf16[2,512,512]{2,1,0:T(8,128)(2,1)S(1)}, bf16[2,512,512]{2,1,0:T(8,128)(2,1)}, u32[]{:S(2)}) copy-start(bf16[2,512,512]{2,1,0:T(8,128)(2,1)} %constant.7.clone.along_hbm) | copy-start | bytes 3145732
  3.1 1.0 %copy-start.2 = (bf16[16,32,512]{2,1,0:T(8,128)(2,1)S(1)}, bf16[16,32,512]{2,1,0:T(8,128)(2,1)}, u32[]{:S(2)}) copy-start(bf16[16,32,512]{2,1,0:T(8,128)(2,1)} %rate_hbm.1) | copy-start | bytes 1572868
  4.1 0.9 %copy-start.3 = (bf16[2,256,256]{2,1,0:T(8,128)(2,1)S(1)}, bf16[2,256,256]{2,1,0:T(8,128)(2,1)}, u32[]{:S(2)}) copy-start(bf16[2,256,256]{2,1,0:T(8,128)(2,1)} %constant.8.clone.local_hbm) | copy-start | bytes 786436
  5.1 0.8 %copy-start.4 = (f32[4,32,128]{2,1,0:T(8,128)S(1)}, f32[4,32,128]{2,1,0:T(8,128)}, u32[]{:S(2)}) copy-start(f32[4,32,128]{2,1,0:T(8,128)} %constant.6.clone.weights_hbm.weights) | copy-start | bytes 196612
  5.9 0.8 %copy-start.5 = (f32[32,512]{1,0:T(8,128)S(1)}, f32[32,512]{1,0:T(8,128)}, u32[]{:S(2)}) copy-start(f32[32,512]{1,0:T(8,128)} %inlet_hbm.1) | copy-start | bytes 196612
where the time goes:
time: 49.9 us; the launch traced here: 49.6 us
  Pallas kernels  42.8 us (86%)
  local copies, waits for them, and re-layouts  6.11 us (12%)
  between operations  0.65 us (1%)
    pallas_call x1, Pallas kernels, per_device(): pl.pallas_call(functools.partial(exchange_kernel, n_ax, n_tr, across), ou...  40.6 us
    unnamed x12, local copies, waits for them, and re-layouts  6.11 us
    pallas_call x1, Pallas kernels, per_device(): pl.pallas_call(finish_kernel, grid=(planes // 4,), out_shape=(shape, shap...  2.16 us

commit v1 on v0

--- a/solution.py
+++ b/solution.py
@@ -44,15 +44,15 @@
         a = np.arange(1, rows + 1, dtype=np.float64)
         block = self.kappa * np.exp(-np.abs(a[:, None] - a[None, :]) * theta)
         self.local = halves(np.kron(np.eye(group), block))
-        weights = np.stack(
-            [
-                np.exp(-(rows - a) * theta),
-                np.exp(-(a - 1) * theta),
-                np.exp(-a * theta),
-                np.exp(-(rows + 1 - a) * theta),
-            ]
-        )
-        self.weights = np.repeat(weights[:, :, None], 128, axis=2).astype(np.float32)
+        self.theta = theta
+
+    def fade_down(self, rows, first):
+        row = lax.broadcasted_iota(jnp.int32, (rows, 128), 0)
+        return jnp.exp((row + first).astype(F32) * -self.theta)
+
+    def fade_up(self, rows, last):
+        row = lax.broadcasted_iota(jnp.int32, (rows, 128), 0)
+        return jnp.exp((rows - 1 + last - row).astype(F32) * -self.theta)
 
 
 def dot3(a_high, a_low, b_high, b_low):
@@ -74,24 +74,20 @@
     inlet_hbm,
     along_hbm,
     local_hbm,
-    weights_hbm,
-    gas_hbm,
-    part_hbm,
-    carry_out,
+    gas,
+    part,
+    carry,
     solid,
     rate,
     inlet,
     along,
     local,
-    weights,
     cumul,
     particular,
-    gas,
     right_hi,
     right_lo,
     mid_hi,
     mid_lo,
-    part,
     pieces,
     first,
     maps,
@@ -103,7 +99,6 @@
     ends,
     ends_in,
     load_sem,
-    store_sem,
     send_sem,
     recv_sem,
 ):
@@ -119,7 +114,6 @@
                 (rate_hbm, rate),
                 (solid_hbm, solid),
                 (inlet_hbm, inlet),
-                (weights_hbm, weights),
                 (local_hbm, local),
                 (along_hbm, along),
             ]
@@ -228,7 +222,6 @@
 
     lax.fori_loop(1, n_ax, send_flow, 0)
     inflows[me_ax] = flows[me_ax]
-    loads[3].wait()
     wait_for(inflows, n_ax - 1, recv_sem.at[1])
 
     for h in range(rows // 8):
@@ -238,10 +231,11 @@
                 [inflows[q], inflows[q + 1]], axis=0
             )
 
+    to_last, to_first = across.fade_up(rows, 0), across.fade_down(rows, 0)
+
     def plane_group(g, _):
         for c in range(col_tiles):
             lanes = pl.ds(128 * c, 128)
-            to_last, to_first = weights[0], weights[1]
             totals = []
             for j in range(4):
                 p = g * 4 + j
@@ -280,10 +274,7 @@
     lax.fori_loop(1, n_tr, send_sum, 0)
     sums_in[me_tr] = sums[me_tr]
 
-    gas_copy = pltpu.make_async_copy(gas, gas_hbm, store_sem.at[0])
-    gas_copy.start()
-
-    loads[4].wait()
+    loads[3].wait()
     group = local.shape[1]
 
     def local_solve(g, _):
@@ -330,7 +321,7 @@
     lax.fori_loop(1, n_tr, send_end, 0)
     ends_box(me_tr)[...] = ends[me_tr]
 
-    loads[5].wait()
+    loads[4].wait()
 
     def along_solve(g, _):
         at = pl.ds(pl.multiple_of(g * group, group), group)
@@ -338,27 +329,23 @@
         return 0
 
     lax.fori_loop(0, planes * rows // group, along_solve, 0)
-    part_copy = pltpu.make_async_copy(part, part_hbm, store_sem.at[1])
-    part_copy.start()
 
     wait_for(ends, n_tr - 1, recv_sem.at[3])
     end_hi, end_lo = split(ends_in[...])
-    carry_out[...] = dot3(end_hi, end_lo, along[0], along[1])
-
-    gas_copy.wait()
-    part_copy.wait()
+    carry[...] = dot3(end_hi, end_lo, along[0], along[1])
+
     wait_for(pieces, n_ax - 1, send_sem.at[0])
     wait_for(flows, n_ax - 1, send_sem.at[1])
     wait_for(sums, n_tr - 1, send_sem.at[2])
     wait_for(ends, n_tr - 1, send_sem.at[3])
 
 
-def finish_kernel(gas_in, part, carry, weights, gas_out, solid_out, gap_out):
+def finish_kernel(across, gas_in, part, carry, gas_out, solid_out, gap_out):
     rows = part.shape[1]
     cols = part.shape[2]
     lanes_of = cols // 128
-    before = jnp.concatenate([weights[2]] * lanes_of, axis=1)
-    after = jnp.concatenate([weights[3]] * lanes_of, axis=1)
+    before = jnp.concatenate([across.fade_down(rows, 1)] * lanes_of, axis=1)
+    after = jnp.concatenate([across.fade_up(rows, 1)] * lanes_of, axis=1)
     for j in range(4):
         new = gas_in[j]
         solid = part[j] + (
@@ -370,38 +357,38 @@
         gap_out[j] = new - solid
 
 
+def far(value):
+    return pltpu.with_memory_space_constraint(value, pltpu.HBM)
+
+
 def per_device(n_ax, n_tr, solid_old, gas_rate, gas_inlet):
     planes, rows, cols = solid_old.shape
     across = Across(rows, n_tr, ACROSS_ROWS, 8)
     along = halves(line_inverse(cols, ALONG_ROW).T)
-    weights = jnp.asarray(across.weights)
     tiles = cols // 128
     anywhere = pl.BlockSpec(memory_space=pl.ANY)
     cells = planes * rows
     gas, part, carry = pl.pallas_call(
         functools.partial(exchange_kernel, n_ax, n_tr, across),
         out_shape=(
-            jax.ShapeDtypeStruct((planes, rows, cols), F32),
-            jax.ShapeDtypeStruct((cells, cols), F32),
-            jax.ShapeDtypeStruct((planes // 4 * 8, cols), F32),
+            pltpu.VMEM((planes, rows, cols), F32),
+            pltpu.VMEM((cells, cols), F32),
+            pltpu.VMEM((planes // 4 * 8, cols), F32),
         ),
-        in_specs=[anywhere] * 6,
-        out_specs=(anywhere, anywhere, pl.BlockSpec(memory_space=pltpu.VMEM)),
+        in_specs=[anywhere] * 5,
+        out_specs=[pl.BlockSpec(memory_space=pltpu.VMEM)] * 3,
         scratch_shapes=[
             pltpu.VMEM((planes, rows, cols), F32),
             pltpu.VMEM((planes, rows, cols), BF16),
             pltpu.VMEM((rows, cols), F32),
             pltpu.VMEM((2, cols, cols), BF16),
             pltpu.VMEM(across.local.shape, BF16),
-            pltpu.VMEM((4, rows, 128), F32),
-            pltpu.VMEM((planes, rows, cols), F32),
             pltpu.VMEM((planes, rows, cols), F32),
             pltpu.VMEM((planes, rows, cols), F32),
             pltpu.VMEM((cells, cols), BF16),
             pltpu.VMEM((cells, cols), BF16),
             pltpu.VMEM((cells, cols), BF16),
             pltpu.VMEM((cells, cols), BF16),
-            pltpu.VMEM((cells, cols), F32),
             pltpu.VMEM((n_ax, 8, 128), F32),
             pltpu.VMEM((n_ax, 8, 128), F32),
             pltpu.VMEM((n_ax, 8, 128), F32),
@@ -412,8 +399,7 @@
             pltpu.VMEM((n_tr, 8, 128), F32),
             pltpu.VMEM((n_tr, 8, 128), F32),
             pltpu.VMEM((planes // 4 * 8, cols), F32),
-            pltpu.SemaphoreType.DMA((6,)),
-            pltpu.SemaphoreType.DMA((2,)),
+            pltpu.SemaphoreType.DMA((5,)),
             pltpu.SemaphoreType.DMA((4,)),
             pltpu.SemaphoreType.DMA((4,)),
         ],
@@ -421,24 +407,23 @@
             collective_id=0, has_side_effects=True, vmem_limit_bytes=32 * 2**20
         ),
         name="exchange",
-    )(solid_old, gas_rate, gas_inlet, jnp.asarray(along), jnp.asarray(across.local), weights)
+    )(*map(far, (solid_old, gas_rate, gas_inlet, jnp.asarray(along), jnp.asarray(across.local))))
 
     field = pl.BlockSpec((4, rows, cols), lambda g: (g, 0, 0))
     shape = jax.ShapeDtypeStruct((planes, rows, cols), F32)
     return pl.pallas_call(
-        finish_kernel,
+        functools.partial(finish_kernel, across),
         grid=(planes // 4,),
         out_shape=(shape, shape, shape),
         in_specs=[
             field,
             field,
             pl.BlockSpec((8, cols), lambda g: (g, 0)),
-            pl.BlockSpec((4, rows, 128), lambda g: (0, 0, 0)),
         ],
         out_specs=(field, field, field),
         compiler_params=pltpu.CompilerParams(vmem_limit_bytes=32 * 2**20),
         name="finish",
-    )(gas, part.reshape(planes, rows, cols), carry, weights)
+    )(gas, part.reshape(planes, rows, cols), carry)
 
 
 def solution(mesh):

time: 49.9 us -> 43.2 us (0.87)
  local copies, waits for them, and re-layouts: 6.11 us -> 0 us
    unnamed x12 -> x0, local copies, waits for them, and re-layouts: 6.11 us -> none
where the time goes in v1:
time: 43.2 us; the launch traced here: 43 us
  Pallas kernels  42.4 us (98%)
  between operations  0.64 us (1%)
    pallas_call x1, Pallas kernels, per_device(): pl.pallas_call(functools.partial(exchange_kernel, n_ax, n_tr, across), ou...  40.2 us
    pallas_call x1, Pallas kernels, per_device(): pl.pallas_call(functools.partial(finish_kernel, across), grid=(planes //...  2.17 us

profile of v1, /device:TPU:1, one launch (start us, length us, event | category | flops | bytes accessed | tf_op | source)
XLA Modules:
  0.0 43.0 jit_solution(14040686240844159234)
XLA Ops:
  0.6 40.2 %exchange.1 = (f32[16,32,512]{2,1,0:T(8,128)S(1)}, f32[512,512]{1,0:T(8,128)S(1)}, f32[32,512]{1,0:T(8,128)S(1)}) custom-call(f32[16,32,512]{2,1,0:T(8,128)} %solid_hbm.1, bf16[16,32,512]{2,1,0:T(8,128)(2,1)} %rate_hbm.1, f32[32,512]{1,0:T(8,128)} %inlet_hbm.1, bf16[2,512,512]{2,1,0:T(8,128)(2,1)} %constant.4.clone.along_hbm, ...), custom_call_target="tpu_custom_call" | custom-call | tf_op jit(solution)/shard_map/exchange/pallas_call | solution.py:371
  40.9 2.2 %finish.1 = (f32[16,32,512]{2,1,0:T(8,128)}, f32[16,32,512]{2,1,0:T(8,128)}, f32[16,32,512]{2,1,0:T(8,128)}) custom-call(f32[16,32,512]{2,1,0:T(8,128)S(1)} %get-tuple-element.6.gas_in, f32[16,32,512]{2,1,0:T(8,128)S(1)} %bitcast.1, f32[32,512]{1,0:T(8,128)S(1)} %get-tuple-element.8.carry), custom_call_target="tpu_custom_call" | custom-call | tf_op jit(solution)/shard_map/finish/pallas_call | solution.py:414

commit v2 on v1

v2 whole, which is shorter than its diff:
```python
import functools
import math

import jax
import jax.numpy as jnp
import ml_dtypes
import numpy as np
from jax import lax
from jax.experimental import pallas as pl
from jax.experimental.pallas import tpu as pltpu
from jax.sharding import PartitionSpec as P

COUPLE = 8.0
ALONG_ROW = 100.0
ACROSS_ROWS = 4000.0
MESH = pl.DeviceIdType.MESH
F32 = jnp.float32
BF16 = jnp.bfloat16


def halves(table):
    high = table.astype(np.float32).astype(ml_dtypes.bfloat16)
    low = (table - high.astype(np.float64)).astype(np.float32).astype(ml_dtypes.bfloat16)
    return np.stack([high, low])


def line_inverse(order_n, conduct):
    theta = 2.0 * math.asinh(0.5 / math.sqrt(conduct))
    i = np.arange(1, order_n + 1, dtype=np.float64)
    near = np.minimum(i[:, None], i[None, :])
    far = order_n + 1 - np.maximum(i[:, None], i[None, :])
    return np.sinh(near * theta) * np.sinh(far * theta) / (
        conduct * math.sinh(theta) * math.sinh((order_n + 1) * theta)
    )


class Across:
    def __init__(self, rows, blocks, conduct, group):
        self.rows = rows
        self.last = rows * blocks + 1
        self.theta = 2.0 * math.asinh(0.5 / math.sqrt(conduct))
        kappa = 1.0 / (2.0 * conduct * math.sinh(self.theta))
        a = np.arange(1, rows + 1, dtype=np.float64)
        block = kappa * np.exp(-np.abs(a[:, None] - a[None, :]) * self.theta)
        self.local = halves(np.kron(np.eye(group), block))
        self.pair = 0.5 / (conduct * math.sinh(self.theta) * math.sinh(self.last * self.theta))
        end = math.exp(-self.last * self.theta)
        self.near = -kappa / (1.0 - end**2)
        self.cross = kappa * end / (1.0 - end**2) * math.exp(-(self.last - rows) * self.theta)

    def fade_down(self, first):
        row = lax.broadcasted_iota(jnp.int32, (self.rows, 128), 0)
        return jnp.exp((row + first).astype(F32) * -self.theta)

    def fade_up(self, last):
        row = lax.broadcasted_iota(jnp.int32, (self.rows, 128), 0)
        return jnp.exp((self.rows - 1 + last - row).astype(F32) * -self.theta)

    def power(self, steps, lanes):
        return jnp.exp(jnp.full((8, lanes), steps, jnp.int32).astype(F32) * self.theta)

    def sums(self, block, to_last, to_first):
        rows, lanes = self.rows, to_last.shape[1]
        power = functools.partial(self.power, lanes=lanes)
        before = rows * block
        return (
            0.5 * (power(before + rows) * to_last - power(-before - 1) * to_first),
            0.5
            * (
                power(self.last - before - 1) * to_first
                - power(before + rows - self.last) * to_last
            ),
        )

    def fields(self, block, below, above, to_last, to_first):
        rows, lanes = self.rows, to_last.shape[1]
        power = functools.partial(self.power, lanes=lanes)
        before = rows * block
        return (
            self.pair * (power(self.last - before) * below - power(-before) * above)
            + self.cross * to_last
            + self.near * power(-2 * before - 1) * to_first,
            self.pair
            * (power(before + rows + 1) * above - power(before + rows + 1 - self.last) * below)
            + self.cross * to_first
            + self.near * power(2 * before + 2 * rows + 1 - 2 * self.last) * to_last,
        )


def dot3(a_high, a_low, b_high, b_low):
    dot = functools.partial(jnp.dot, preferred_element_type=F32)
    return dot(a_high, b_high) + (dot(a_low, b_high) + dot(a_high, b_low))


def split(value):
    high = value.astype(BF16)
    return high, (value - high.astype(F32)).astype(BF16)


def exchange_kernel(
    n_ax,
    n_tr,
    across,
    solid_hbm,
    rate_hbm,
    inlet_hbm,
    along_hbm,
    local_hbm,
    gas,
    part,
    carry,
    solid,
    rate,
    inlet,
    along,
    local,
    cumul,
    particular,
    right_hi,
    right_lo,
    mid_hi,
    mid_lo,
    pieces,
    maps,
    flows,
    inflow,
    own,
    sums,
    sums_in,
    twin_out,
    pairs,
    load_sem,
    send_sem,
    recv_sem,
):
    me_ax = lax.axis_index("ax")
    me_tr = lax.axis_index("tr")
    planes, rows, cols = solid.shape
    col_tiles = cols // 128
    half = planes // 2
    n_owner = pieces.shape[0]
    is_owner = me_ax < n_owner
    my_piece = jnp.where(is_owner, me_ax, 0)
    core = lax.rem(me_tr, 2)
    twin = me_tr + 1 - 2 * core

    first_rows, last_rows = pl.ds(0, rows // 2), pl.ds(rows // 2, rows // 2)
    loads = [
        pltpu.make_async_copy(source, target, load_sem.at[i])
        for i, (source, target) in enumerate(
            [
                (rate_hbm.at[:, first_rows], rate.at[:, first_rows]),
                (solid_hbm.at[:, first_rows], solid.at[:, first_rows]),
                (rate_hbm.at[:, last_rows], rate.at[:, last_rows]),
                (solid_hbm.at[:, last_rows], solid.at[:, last_rows]),
                (inlet_hbm, inlet),
                (local_hbm, local),
                (along_hbm, along),
            ]
        )
    ]
    for load in loads[:5]:
        load.start()

    barrier = pltpu.get_barrier_semaphore()

    def greet(ax, tr):
        pl.semaphore_signal(barrier, inc=1, device_id=(ax, tr), device_id_type=MESH)

    @pl.when(is_owner)
    def _():
        def one(k, _):
            greet(lax.rem(me_ax + k, n_ax), me_tr)
            return 0

        lax.fori_loop(1, n_ax, one, 0)

    def greet_tr(k, _):
        greet(me_ax, lax.rem(me_tr + k, n_tr))
        return 0

    lax.fori_loop(1, n_tr, greet_tr, 0)

    for g in range(2):
        loads[2 * g].wait()
        loads[2 * g + 1].wait()
        if g == 1:
            loads[4].wait()
            loads[5].start()
            loads[6].start()
        at = pl.ds(g * 16, 16)

        def plane(p, state, at=at):
            factor, offset = state
            r = rate[p, at, :].astype(F32)
            near_keep = pl.reciprocal(1.0 + r, approx=True)
            keep = near_keep * (2.0 - (1.0 + r) * near_keep)
            factor = factor * keep
            offset = (offset + r * solid[p, at, :]) * keep
            cumul[p, at, :] = factor
            particular[p, at, :] = offset
            return factor, offset

        factor, offset = lax.fori_loop(
            0,
            planes,
            plane,
            (jnp.ones((16, cols), F32), jnp.zeros((16, cols), F32)),
            unroll=True,
        )
        for h in range(2):
            for c in range(col_tiles):
                box = (slice(8 * h, 8 * h + 8), slice(128 * c, 128 * c + 128))
                q = (g * 2 + h) * col_tiles + c
                pieces[q, 0] = factor[box]
                pieces[q, 1] = offset[box]

    pl.semaphore_wait(barrier, jnp.where(is_owner, n_owner - 1, n_owner) + n_tr - 1)

    def send_map(k, _):
        to = lax.rem(me_ax + k, n_owner)

        @pl.when(to != me_ax)
        def _():
            pltpu.make_async_remote_copy(
                src_ref=pieces.at[to],
                dst_ref=maps.at[me_ax],
                send_sem=send_sem.at[0],
                recv_sem=recv_sem.at[0],
                device_id=(to, me_tr),
                device_id_type=MESH,
            ).start()

        return 0

    lax.fori_loop(0, n_owner, send_map, 0)

    def wait_for(ref, count, sem):
        box = ref.at[pl.ds(0, count)]
        pltpu.make_async_copy(box, box, sem).wait()

    def tile_of(ref, piece):
        return ref.at[
            pl.ds(pl.multiple_of(piece // col_tiles * 8, 8), 8),
            pl.ds(pl.multiple_of(lax.rem(piece, col_tiles) * 128, 128), 128),
        ]

    @pl.when(is_owner)
    def _():
        maps[me_ax] = pieces[my_piece]
        wait_for(maps, n_ax - 1, recv_sem.at[0])

        def march(k, state):
            flows[k] = state
            return maps[k, 0] * state + maps[k, 1]

        lax.fori_loop(0, n_ax, march, tile_of(inlet, my_piece)[...], unroll=True)

        def send_flow(k, _):
            to = lax.rem(k, 4) * 8 + k // 4

            @pl.when(to != me_ax)
            def _():
                pltpu.make_async_remote_copy(
                    src_ref=flows.at[to],
                    dst_ref=tile_of(inflow, my_piece),
                    send_sem=send_sem.at[1],
                    recv_sem=recv_sem.at[1],
                    device_id=(to, me_tr),
                    device_id_type=MESH,
                ).start()

            return 0

        lax.fori_loop(0, n_ax, send_flow, 0)
        tile_of(inflow, my_piece)[...] = flows[me_ax]
        wait_for(flows, n_owner - 1, recv_sem.at[1])

    @pl.when(jnp.logical_not(is_owner))
    def _():
        wait_for(flows, n_owner, recv_sem.at[1])

    def send_sum(to):
        pltpu.make_async_remote_copy(
            src_ref=sums.at[lax.rem(to, 2), (to < me_tr).astype(jnp.int32)],
            dst_ref=sums_in.at[me_tr],
            send_sem=send_sem.at[2],
            recv_sem=recv_sem.at[2],
            device_id=(me_ax, to),
            device_id_type=MESH,
        ).start()

    def plane_group(g, _):
        to_last, to_first = across.fade_up(0), across.fade_down(0)
        for c in range(col_tiles):
            lanes = pl.ds(128 * c, 128)
            totals = []
            for j in range(half):
                p = g * half + j
                s = solid[p, :, lanes]
                r = rate[p, :, lanes].astype(F32)
                new = particular[p, :, lanes] + cumul[p, :, lanes] * inflow[:, lanes]
                gas[p, :, lanes] = new
                right = s + (COUPLE * r) * (new - s)
                at = pl.ds(pl.multiple_of(p * rows, rows), rows)
                right_hi[at, lanes], right_lo[at, lanes] = split(right)
                totals.append(
                    (
                        jnp.sum(right * to_last, axis=0, keepdims=True),
                        jnp.sum(right * to_first, axis=0, keepdims=True),
                    )
                )
            last = jnp.concatenate([t[0] for t in totals], axis=0)
            start = jnp.concatenate([t[1] for t in totals], axis=0)
            own[g, 0, :, lanes], own[g, 1, :, lanes] = last, start
            sums[g, 0, :, lanes], sums[g, 1, :, lanes] = across.sums(me_tr, last, start)

        def send(k, _):
            to = 2 * k + g

            @pl.when(to != me_tr)
            def _():
                send_sum(to)

            return 0

        lax.fori_loop(0, n_tr // 2, send, 0)
        return 0

    lax.fori_loop(0, 2, plane_group, 0)
    sums_in[me_tr] = sums[core, core]

    loads[5].wait()
    loads[6].wait()
    group = local.shape[1]

    def own_solve(g, _):
        at = pl.ds(pl.multiple_of(g * group, group), group)
        mid = dot3(local[0], local[1], right_hi[at, :], right_lo[at, :])
        mid_hi[at, :], mid_lo[at, :] = split(mid)
        part[at, :] = dot3(mid_hi[at, :], mid_lo[at, :], along[0], along[1])
        return 0

    lax.fori_loop(0, planes * rows // group, own_solve, 0)

    wait_for(sums_in, n_tr - 1, recv_sem.at[2])

    nothing = jnp.zeros((half, cols), F32)

    def add(k, totals):
        value = sums_in[k]
        return tuple(
            total + jnp.where(test, value, 0.0)
            for total, test in zip(totals, (k < me_tr, k > me_tr, k < twin, k > twin))
        )

    mine = lax.fori_loop(0, n_tr, add, (nothing,) * 4, unroll=True)
    twin_out[0], twin_out[1] = mine[2], mine[3]
    to_twin = pltpu.make_async_remote_copy(
        src_ref=twin_out,
        dst_ref=pairs.at[core],
        send_sem=send_sem.at[3],
        recv_sem=recv_sem.at[3],
        device_id=(me_ax, twin),
        device_id_type=MESH,
    )
    to_twin.start()
    pairs[core, 0], pairs[core, 1] = mine[0], mine[1]

    to_twin.wait_recv()
    fields = []
    for g in range(2):
        fields.extend(
            across.fields(me_tr, pairs[g, 0], pairs[g, 1], own[g, 0], own[g, 1])
        )
    end_hi, end_lo = split(jnp.concatenate(fields, axis=0))
    carry[...] = dot3(end_hi, end_lo, along[0], along[1])

    to_twin.wait_send()
    wait_for(sums_in, n_tr - 1, send_sem.at[2])

    @pl.when(is_owner)
    def _():
        wait_for(pieces, n_owner - 1, send_sem.at[0])
        wait_for(flows, n_ax - 1, send_sem.at[1])

    @pl.when(jnp.logical_not(is_owner))
    def _():
        wait_for(pieces, n_owner, send_sem.at[0])


def finish_kernel(across, gas, part, carry, gas_hbm, solid_hbm, gap_hbm, solid, gap, store_sem):
    planes, rows, cols = gas.shape
    half = planes // 2
    gas_store = pltpu.make_async_copy(gas, gas_hbm, store_sem.at[0, 0])
    gas_store.start()
    before = jnp.concatenate([across.fade_down(1)] * (cols // 128), axis=1)
    after = jnp.concatenate([across.fade_up(1)] * (cols // 128), axis=1)
    stores = []
    for p in range(planes):
        row = p // half * planes + p % half
        new = part[p] + (
            before * jnp.broadcast_to(carry[row : row + 1, :], (rows, cols))
            + after * jnp.broadcast_to(carry[row + half : row + half + 1, :], (rows, cols))
        )
        solid[p] = new
        gap[p] = gas[p] - new
        if p % 2 == 1:
            for i, (source, target) in enumerate(((solid, solid_hbm), (gap, gap_hbm))):
                box = pl.ds(p - 1, 2)
                stores.append(
                    pltpu.make_async_copy(
                        source.at[box], target.at[box], store_sem.at[1 + i, p // 2]
                    )
                )
                stores[-1].start()
    gas_store.wait()
    for store in stores:
        store.wait()


def far(value):
    return pltpu.with_memory_space_constraint(value, pltpu.HBM)


def per_device(n_ax, n_tr, solid_old, gas_rate, gas_inlet):
    planes, rows, cols = solid_old.shape
    across = Across(rows, n_tr, ACROSS_ROWS, 8)
    along = halves(line_inverse(cols, ALONG_ROW).T)
    cells = planes * rows
    half = planes // 2
    pieces = (rows // 8) * (cols // 128)
    field = (planes, rows, cols)
    anywhere = pl.BlockSpec(memory_space=pl.ANY)
    near = pl.BlockSpec(memory_space=pltpu.VMEM)
    gas, part, carry = pl.pallas_call(
        functools.partial(exchange_kernel, n_ax, n_tr, across),
        out_shape=(
            pltpu.VMEM(field, F32),
            pltpu.VMEM((cells, cols), F32),
            pltpu.VMEM((2 * planes, cols), F32),
        ),
        in_specs=[anywhere] * 5,
        out_specs=[near] * 3,
        scratch_shapes=[
            pltpu.VMEM(field, F32),
            pltpu.VMEM(field, BF16),
            pltpu.VMEM((rows, cols), F32),
            pltpu.VMEM((2, cols, cols), BF16),
            pltpu.VMEM(across.local.shape, BF16),
            pltpu.VMEM(field, F32),
            pltpu.VMEM(field, F32),
            pltpu.VMEM((cells, cols), BF16),
            pltpu.VMEM((cells, cols), BF16),
            pltpu.VMEM((cells, cols), BF16),
            pltpu.VMEM((cells, cols), BF16),
            pltpu.VMEM((pieces, 2, 8, 128), F32),
            pltpu.VMEM((n_ax, 2, 8, 128), F32),
            pltpu.VMEM((n_ax, 8, 128), F32),
            pltpu.VMEM((rows, cols), F32),
            pltpu.VMEM((2, 2, half, cols), F32),
            pltpu.VMEM((2, 2, half, cols), F32),
            pltpu.VMEM((n_tr, half, cols), F32),
            pltpu.VMEM((2, half, cols), F32),
            pltpu.VMEM((2, 2, half, cols), F32),
            pltpu.SemaphoreType.DMA((7,)),
            pltpu.SemaphoreType.DMA((4,)),
            pltpu.SemaphoreType.DMA((4,)),
        ],
        compiler_params=pltpu.CompilerParams(
            collective_id=0, has_side_effects=True, vmem_limit_bytes=32 * 2**20
        ),
        name="exchange",
    )(*map(far, (solid_old, gas_rate, gas_inlet, jnp.asarray(along), jnp.asarray(across.local))))

    shape = jax.ShapeDtypeStruct(field, F32)
    return pl.pallas_call(
        functools.partial(finish_kernel, across),
        out_shape=(shape, shape, shape),
        in_specs=[near] * 3,
        out_specs=[anywhere] * 3,
        scratch_shapes=[
            pltpu.VMEM(field, F32),
            pltpu.VMEM(field, F32),
            pltpu.SemaphoreType.DMA((3, planes // 2)),
        ],
        compiler_params=pltpu.CompilerParams(vmem_limit_bytes=16 * 2**20),
        name="finish",
    )(gas, part.reshape(field), carry)


def solution(mesh):
    n_ax, n_tr = mesh.shape["ax"], mesh.shape["tr"]
    return jax.shard_map(
        functools.partial(per_device, n_ax, n_tr),
        mesh=mesh,
        in_specs=(P("ax", "tr", None), P("ax", "tr", None), P("tr", None)),
        out_specs=(P("ax", "tr", None), P("ax", "tr", None), P("ax", "tr", None)),
        check_vma=False,
    )
```

time: 43.2 us -> 38 us (0.88)
  Pallas kernels: 42.4 us -> 37.3 us
    pallas_call x1, Pallas kernels: 40.2 us -> 35.4 us  [per_device(): pl.pallas_call(functools.partial(exchange_kernel, n_ax, n_tr, across), ou...]
where the time goes in v2:
time: 38 us; the launch traced here: 37.9 us
  Pallas kernels  37.3 us (98%)
  between operations  0.64 us (2%)
    pallas_call x1, Pallas kernels, per_device(): pl.pallas_call(functools.partial(exchange_kernel, n_ax, n_tr, across), ou...  35.4 us
    pallas_call x1, Pallas kernels, per_device(): pl.pallas_call(functools.partial(finish_kernel, across), out_shape=(shape...  1.86 us

profile of v2, /device:TPU:1, one launch (start us, length us, event | category | flops | bytes accessed | tf_op | source)
XLA Modules:
  0.0 37.9 jit_solution(676241985831459709)
XLA Ops:
  0.6 35.4 %exchange.1 = (f32[16,32,512]{2,1,0:T(8,128)S(1)}, f32[512,512]{1,0:T(8,128)S(1)}, f32[32,512]{1,0:T(8,128)S(1)}) custom-call(f32[16,32,512]{2,1,0:T(8,128)} %solid_hbm.1, bf16[16,32,512]{2,1,0:T(8,128)(2,1)} %rate_hbm.1, f32[32,512]{1,0:T(8,128)} %inlet_hbm.1, bf16[2,512,512]{2,1,0:T(8,128)(2,1)} %constant.4.clone.along_hbm, ...), custom_call_target="tpu_custom_call" | custom-call | tf_op jit(solution)/shard_map/exchange/pallas_call | solution.py:436
  36.0 1.9 %finish.1 = (f32[16,32,512]{2,1,0:T(8,128)}, f32[16,32,512]{2,1,0:T(8,128)}, f32[16,32,512]{2,1,0:T(8,128)}) custom-call(f32[16,32,512]{2,1,0:T(8,128)S(1)} %get-tuple-element.6.gas, f32[16,32,512]{2,1,0:T(8,128)S(1)} %bitcast.1, f32[32,512]{1,0:T(8,128)S(1)} %get-tuple-element.8.carry), custom_call_target="tpu_custom_call" | custom-call | tf_op jit(solution)/shard_map/finish/pallas_call | solution.py:477

commit v3 on v2

--- a/solution.py
+++ b/solution.py
@@ -57,7 +57,8 @@
         return jnp.exp((self.rows - 1 + last - row).astype(F32) * -self.theta)
 
     def power(self, steps, lanes):
-        return jnp.exp(jnp.full((8, lanes), steps, jnp.int32).astype(F32) * self.theta)
+        tile = jnp.exp(jnp.full((8, 128), steps, jnp.int32).astype(F32) * self.theta)
+        return jnp.concatenate([tile] * (lanes // 128), axis=1)
 
     def sums(self, block, to_last, to_first):
         rows, lanes = self.rows, to_last.shape[1]
@@ -95,6 +96,21 @@
 def split(value):
     high = value.astype(BF16)
     return high, (value - high.astype(F32)).astype(BF16)
+
+
+def row_sums(values):
+    values = [sum(v[i : i + 8] for i in range(8, v.shape[0], 8)) + v[:8] for v in values]
+    row = lax.broadcasted_iota(jnp.int32, values[0].shape, 0)
+    step = 4
+    while step:
+        low = (row & step) == 0
+        count = len(values) // 2
+        values = [
+            jnp.where(low, a, pltpu.roll(b, step, 0)) + jnp.where(low, pltpu.roll(a, 8 - step, 0), b)
+            for a, b in zip(values[:count], values[count:])
+        ]
+        step //= 2
+    return values[0]
 
 
 def exchange_kernel(
@@ -116,6 +132,8 @@
     local,
     cumul,
     particular,
+    still,
+    driven,
     right_hi,
     right_lo,
     mid_hi,
@@ -139,8 +157,15 @@
     col_tiles = cols // 128
     half = planes // 2
     n_owner = pieces.shape[0]
-    is_owner = me_ax < n_owner
-    my_piece = jnp.where(is_owner, me_ax, 0)
+    ring, place = me_ax // 8, lax.rem(me_ax, 8)
+    wide = jnp.logical_and(ring < 2, place != 4)
+    is_owner = jnp.logical_or(wide, jnp.logical_and(ring == 2, place < 2))
+    my_piece = jnp.where(wide, ring * 7 + lax.rem(place + 3, 8), jnp.where(is_owner, 14 + place, 0))
+
+    def owner_of(piece):
+        wide_at = piece // 7 * 8 + lax.rem(lax.rem(piece, 7) + 5, 8)
+        return jnp.where(piece < 14, wide_at, piece + 2)
+
     core = lax.rem(me_tr, 2)
     twin = me_tr + 1 - 2 * core
 
@@ -218,12 +243,13 @@
     pl.semaphore_wait(barrier, jnp.where(is_owner, n_owner - 1, n_owner) + n_tr - 1)
 
     def send_map(k, _):
-        to = lax.rem(me_ax + k, n_owner)
+        piece = lax.rem(me_ax + k, n_owner)
+        to = owner_of(piece)
 
         @pl.when(to != me_ax)
         def _():
             pltpu.make_async_remote_copy(
-                src_ref=pieces.at[to],
+                src_ref=pieces.at[piece],
                 dst_ref=maps.at[me_ax],
                 send_sem=send_sem.at[0],
                 recv_sem=recv_sem.at[0],
@@ -234,6 +260,25 @@
         return 0
 
     lax.fori_loop(0, n_owner, send_map, 0)
+
+    to_last, to_first = across.fade_up(0), across.fade_down(0)
+
+    def prepare(g, _):
+        for c in range(col_tiles):
+            lanes = pl.ds(128 * c, 128)
+            values = []
+            for j in range(half):
+                p = g * half + j
+                s = solid[p, :, lanes]
+                r = COUPLE * rate[p, :, lanes].astype(F32)
+                driven[p, :, lanes] = r * cumul[p, :, lanes]
+                values.append(s + r * (particular[p, :, lanes] - s))
+                still[p, :, lanes] = values[-1]
+            own[g, 0, :, lanes] = row_sums([v * to_last for v in values])
+            own[g, 1, :, lanes] = row_sums([v * to_first for v in values])
+        return 0
+
+    lax.fori_loop(0, 2, prepare, 0)
 
     def wait_for(ref, count, sem):
         box = ref.at[pl.ds(0, count)]
@@ -290,45 +335,37 @@
             device_id_type=MESH,
         ).start()
 
-    def plane_group(g, _):
-        to_last, to_first = across.fade_up(0), across.fade_down(0)
+    def add_inflow(g, _):
         for c in range(col_tiles):
             lanes = pl.ds(128 * c, 128)
-            totals = []
-            for j in range(half):
-                p = g * half + j
-                s = solid[p, :, lanes]
-                r = rate[p, :, lanes].astype(F32)
-                new = particular[p, :, lanes] + cumul[p, :, lanes] * inflow[:, lanes]
-                gas[p, :, lanes] = new
-                right = s + (COUPLE * r) * (new - s)
-                at = pl.ds(pl.multiple_of(p * rows, rows), rows)
-                right_hi[at, lanes], right_lo[at, lanes] = split(right)
-                totals.append(
-                    (
-                        jnp.sum(right * to_last, axis=0, keepdims=True),
-                        jnp.sum(right * to_first, axis=0, keepdims=True),
-                    )
-                )
-            last = jnp.concatenate([t[0] for t in totals], axis=0)
-            start = jnp.concatenate([t[1] for t in totals], axis=0)
+            flow = inflow[:, lanes]
+            down, up = flow * to_last, flow * to_first
+            values = [driven[g * half + j, :, lanes] for j in range(half)]
+            last = own[g, 0, :, lanes] + row_sums([v * down for v in values])
+            start = own[g, 1, :, lanes] + row_sums([v * up for v in values])
             own[g, 0, :, lanes], own[g, 1, :, lanes] = last, start
             sums[g, 0, :, lanes], sums[g, 1, :, lanes] = across.sums(me_tr, last, start)
-
-        def send(k, _):
-            to = 2 * k + g
-
-            @pl.when(to != me_tr)
-            def _():
-                send_sum(to)
-
-            return 0
-
-        lax.fori_loop(0, n_tr // 2, send, 0)
-        return 0
-
-    lax.fori_loop(0, 2, plane_group, 0)
+        return 0
+
+    lax.fori_loop(0, 2, add_inflow, 0)
+
+    def send(to, _):
+        @pl.when(to != me_tr)
+        def _():
+            send_sum(to)
+
+        return 0
+
+    lax.fori_loop(0, n_tr, send, 0)
     sums_in[me_tr] = sums[core, core]
+
+    def finish_plane(p, _):
+        gas[p] = particular[p] + cumul[p] * inflow[...]
+        at = pl.ds(pl.multiple_of(p * rows, rows), rows)
+        right_hi[at, :], right_lo[at, :] = split(still[p] + driven[p] * inflow[...])
+        return 0
+
+    lax.fori_loop(0, planes, finish_plane, 0, unroll=2)
 
     loads[5].wait()
     loads[6].wait()
@@ -448,6 +485,8 @@
             pltpu.VMEM((rows, cols), F32),
             pltpu.VMEM((2, cols, cols), BF16),
             pltpu.VMEM(across.local.shape, BF16),
+            pltpu.VMEM(field, F32),
+            pltpu.VMEM(field, F32),
             pltpu.VMEM(field, F32),
             pltpu.VMEM(field, F32),
             pltpu.VMEM((cells, cols), BF16),

time: 38 us -> 37.3 us (0.982)
  Pallas kernels: 37.3 us -> 36.5 us
    pallas_call x1, Pallas kernels: 35.4 us -> 34.7 us  [per_device(): pl.pallas_call(functools.partial(exchange_kernel, n_ax, n_tr, across), ou...]
where the time goes in v3:
time: 37.3 us; the launch traced here: 37.2 us
  Pallas kernels  36.5 us (98%)
  between operations  0.64 us (2%)
    pallas_call x1, Pallas kernels, per_device(): pl.pallas_call(functools.partial(exchange_kernel, n_ax, n_tr, across), ou...  34.7 us
    pallas_call x1, Pallas kernels, per_device(): pl.pallas_call(functools.partial(finish_kernel, across), out_shape=(shape...  1.86 us

profile of v3, /device:TPU:1, one launch (start us, length us, event | category | flops | bytes accessed | tf_op | source)
XLA Modules:
  0.0 37.2 jit_solution(17567463980682448675)
XLA Ops:
  0.6 34.7 %exchange.1 = (f32[16,32,512]{2,1,0:T(8,128)S(1)}, f32[512,512]{1,0:T(8,128)S(1)}, f32[32,512]{1,0:T(8,128)S(1)}) custom-call(f32[16,32,512]{2,1,0:T(8,128)} %solid_hbm.1, bf16[16,32,512]{2,1,0:T(8,128)(2,1)} %rate_hbm.1, f32[32,512]{1,0:T(8,128)} %inlet_hbm.1, bf16[2,512,512]{2,1,0:T(8,128)(2,1)} %constant.4.clone.along_hbm, ...), custom_call_target="tpu_custom_call" | custom-call | tf_op jit(solution)/shard_map/exchange/pallas_call | solution.py:473
  35.3 1.9 %finish.1 = (f32[16,32,512]{2,1,0:T(8,128)}, f32[16,32,512]{2,1,0:T(8,128)}, f32[16,32,512]{2,1,0:T(8,128)}) custom-call(f32[16,32,512]{2,1,0:T(8,128)S(1)} %get-tuple-element.6.gas, f32[16,32,512]{2,1,0:T(8,128)S(1)} %bitcast.1, f32[32,512]{1,0:T(8,128)S(1)} %get-tuple-element.8.carry), custom_call_target="tpu_custom_call" | custom-call | tf_op jit(solution)/shard_map/finish/pallas_call | solution.py:516

commit v4 on v3

--- a/solution.py
+++ b/solution.py
@@ -169,6 +169,24 @@
     core = lax.rem(me_tr, 2)
     twin = me_tr + 1 - 2 * core
 
+    barrier = pltpu.get_barrier_semaphore()
+
+    def greet(ax, tr):
+        pl.semaphore_signal(barrier, inc=1, device_id=(ax, tr), device_id_type=MESH)
+
+    @pl.when(is_owner)
+    def _():
+        def one(k, _):
+            to = lax.rem(me_ax + n_ax // 2 - 4 + k, n_ax)
+
+            @pl.when(to != me_ax)
+            def _():
+                greet(to, me_tr)
+
+            return 0
+
+        lax.fori_loop(0, n_ax, one, 0)
+
     first_rows, last_rows = pl.ds(0, rows // 2), pl.ds(rows // 2, rows // 2)
     loads = [
         pltpu.make_async_copy(source, target, load_sem.at[i])
@@ -186,19 +204,6 @@
     ]
     for load in loads[:5]:
         load.start()
-
-    barrier = pltpu.get_barrier_semaphore()
-
-    def greet(ax, tr):
-        pl.semaphore_signal(barrier, inc=1, device_id=(ax, tr), device_id_type=MESH)
-
-    @pl.when(is_owner)
-    def _():
-        def one(k, _):
-            greet(lax.rem(me_ax + k, n_ax), me_tr)
-            return 0
-
-        lax.fori_loop(1, n_ax, one, 0)
 
     def greet_tr(k, _):
         greet(me_ax, lax.rem(me_tr + k, n_tr))

time: 37.3 us -> 36.9 us (0.989)
  Pallas kernels: 36.5 us -> 36.1 us
    pallas_call x1, Pallas kernels: 34.7 us -> 34.3 us  [per_device(): pl.pallas_call(functools.partial(exchange_kernel, n_ax, n_tr, across), ou...]
where the time goes in v4:
time: 36.9 us; the launch traced here: 36.8 us
  Pallas kernels  36.1 us (98%)
  between operations  0.64 us (2%)
    pallas_call x1, Pallas kernels, per_device(): pl.pallas_call(functools.partial(exchange_kernel, n_ax, n_tr, across), ou...  34.3 us
    pallas_call x1, Pallas kernels, per_device(): pl.pallas_call(functools.partial(finish_kernel, across), out_shape=(shape...  1.86 us

profile of v4, /device:TPU:1, one launch (start us, length us, event | category | flops | bytes accessed | tf_op | source)
XLA Modules:
  0.0 36.8 jit_solution(12997862210411443433)
XLA Ops:
  0.6 34.3 %exchange.1 = (f32[16,32,512]{2,1,0:T(8,128)S(1)}, f32[512,512]{1,0:T(8,128)S(1)}, f32[32,512]{1,0:T(8,128)S(1)}) custom-call(f32[16,32,512]{2,1,0:T(8,128)} %solid_hbm.1, bf16[16,32,512]{2,1,0:T(8,128)(2,1)} %rate_hbm.1, f32[32,512]{1,0:T(8,128)} %inlet_hbm.1, bf16[2,512,512]{2,1,0:T(8,128)(2,1)} %constant.4.clone.along_hbm, ...), custom_call_target="tpu_custom_call" | custom-call | tf_op jit(solution)/shard_map/exchange/pallas_call | solution.py:478
  34.9 1.9 %finish.1 = (f32[16,32,512]{2,1,0:T(8,128)}, f32[16,32,512]{2,1,0:T(8,128)}, f32[16,32,512]{2,1,0:T(8,128)}) custom-call(f32[16,32,512]{2,1,0:T(8,128)S(1)} %get-tuple-element.6.gas, f32[16,32,512]{2,1,0:T(8,128)S(1)} %bitcast.1, f32[32,512]{1,0:T(8,128)S(1)} %get-tuple-element.8.carry), custom_call_target="tpu_custom_call" | custom-call | tf_op jit(solution)/shard_map/finish/pallas_call | solution.py:521

commit v5 on v4

--- a/solution.py
+++ b/solution.py
@@ -409,14 +409,15 @@
     to_twin.start()
     pairs[core, 0], pairs[core, 1] = mine[0], mine[1]
 
+    def carry_of(g):
+        at = pl.ds(pl.multiple_of(g * planes, planes), planes)
+        fields = across.fields(me_tr, pairs[g, 0], pairs[g, 1], own[g, 0], own[g, 1])
+        end_hi, end_lo = split(jnp.concatenate(fields, axis=0))
+        carry[at, :] = dot3(end_hi, end_lo, along[0], along[1])
+
+    carry_of(core)
     to_twin.wait_recv()
-    fields = []
-    for g in range(2):
-        fields.extend(
-            across.fields(me_tr, pairs[g, 0], pairs[g, 1], own[g, 0], own[g, 1])
-        )
-    end_hi, end_lo = split(jnp.concatenate(fields, axis=0))
-    carry[...] = dot3(end_hi, end_lo, along[0], along[1])
+    carry_of(1 - core)
 
     to_twin.wait_send()
     wait_for(sums_in, n_tr - 1, send_sem.at[2])

time: 36.9 us -> 36.9 us (level)
  no operation moved by 1% of the time
where the time goes in v5:
time: 36.9 us; the launch traced here: 36.7 us
  Pallas kernels  36.1 us (98%)
  between operations  0.64 us (2%)
    pallas_call x1, Pallas kernels, per_device(): pl.pallas_call(functools.partial(exchange_kernel, n_ax, n_tr, across), ou...  34.2 us
    pallas_call x1, Pallas kernels, per_device(): pl.pallas_call(functools.partial(finish_kernel, across), out_shape=(shape...  1.86 us

profile of v5, /device:TPU:1, one launch (start us, length us, event | category | flops | bytes accessed | tf_op | source)
XLA Modules:
  0.0 36.7 jit_solution(12913477974793531153)
XLA Ops:
  0.6 34.2 %exchange.1 = (f32[16,32,512]{2,1,0:T(8,128)S(1)}, f32[512,512]{1,0:T(8,128)S(1)}, f32[32,512]{1,0:T(8,128)S(1)}) custom-call(f32[16,32,512]{2,1,0:T(8,128)} %solid_hbm.1, bf16[16,32,512]{2,1,0:T(8,128)(2,1)} %rate_hbm.1, f32[32,512]{1,0:T(8,128)} %inlet_hbm.1, bf16[2,512,512]{2,1,0:T(8,128)(2,1)} %constant.4.clone.along_hbm, ...), custom_call_target="tpu_custom_call" | custom-call | tf_op jit(solution)/shard_map/exchange/pallas_call | solution.py:479
  34.9 1.9 %finish.1 = (f32[16,32,512]{2,1,0:T(8,128)}, f32[16,32,512]{2,1,0:T(8,128)}, f32[16,32,512]{2,1,0:T(8,128)}) custom-call(f32[16,32,512]{2,1,0:T(8,128)S(1)} %get-tuple-element.6.gas, f32[16,32,512]{2,1,0:T(8,128)S(1)} %bitcast.1, f32[32,512]{1,0:T(8,128)S(1)} %get-tuple-element.8.carry), custom_call_target="tpu_custom_call" | custom-call | tf_op jit(solution)/shard_map/finish/pallas_call | solution.py:522
